TPU v7x, 32 devices: a whole 2x2x4 slice. The times are simulated.
32 devices in a mesh: batch: 4 (over y, x), ctx: 8 (over z, core).
Axes of the slice: x: 2, y: 2, z: 4, core: 2. Of those that a mesh axis runs over, the one named last changes fastest.
Arguments:
- tokens: bfloat16 [16, 1024, 640], P('batch', 'ctx'), may hold values from -6 to 6
- w_qkv: bfloat16 [640, 1536], P('ctx', 'batch'), may hold values from -0.25 to 0.25
- w_out: bfloat16 [1024, 640], P('batch', 'ctx'), may hold values from -0.1875 to 0.1875
- w_gate_up: bfloat16 [640, 4096], P('ctx', 'batch'), may hold values from -0.25 to 0.25
- w_down: bfloat16 [2048, 640], P('batch', 'ctx'), may hold values from -0.125 to 0.125
- norm_gains: bfloat16 [3072], P(('batch', 'ctx')), may hold values from -0.5 to 0.5
- block_order: int32 [16], replicated, may hold values from 0 to 15, as said below
- cotangent: bfloat16 [16, 1024, 640], P('batch', 'ctx'), may hold values from -6 to 6
Outputs:
- output: bfloat16 [16, 1024, 640], P('batch', 'ctx')
- grad_tokens: float32 [16, 1024, 640], P('batch', 'ctx')
- grad_w_qkv: float32 [640, 1536], P('ctx', 'batch')
- grad_w_out: float32 [1024, 640], P('batch', 'ctx')
- grad_w_gate_up: float32 [640, 4096], P('ctx', 'batch')
- grad_w_down: float32 [2048, 640], P('batch', 'ctx')
- grad_gains: float32 [3072], P(('batch', 'ctx'))
Inputs may be any that keep to these rules, and one draw needn't show every extreme that they name: `block_order`: each block of 0 .. 15 appears once; slots 2c and 2c + 1 hold blocks b and 15 - b.
All inputs are finite; a program needn't handle non-finite values.
Results may differ from a plain program's by a relative error of at most 0.03.
Values may be sent and summed in bfloat16 or wider, within the bound.
A program may use at most 128 MiB of HBM per device.

v0:
```python
import jax
import jax.numpy as jnp
from jax import lax
from jax.sharding import PartitionSpec as P

D = 640
H = 4
HD = 256
FF = 2048


rope_base = 1000000.0
epsilon = 1e-06
neg_large = -1e30


def passed_along(value, axis, steps):
    count = lax.axis_size(axis)
    pairs = [(source, (source + steps) % count) for source in range(count)]
    return lax.ppermute(value, axis, pairs)


def rms_scale(values, gain_vec):
    mean_square = jnp.mean(values * values, axis=-1, keepdims=True)
    return values * lax.rsqrt(mean_square + epsilon) * (1.0 + gain_vec)


def gelu_tanh(values):
    return (
        0.5
        * values
        * (1.0 + jnp.tanh(0.7978845608028654 * (values + 0.044715 * values * values * values)))
    )


def rope_tables(positions, head_size):
    half_size = head_size // 2
    exponent = jnp.arange(half_size, dtype=jnp.float32) * (2.0 / head_size)
    frequency = rope_base ** (-exponent)
    angles = positions.astype(jnp.float32)[:, None] * frequency[None, :]
    return (jnp.cos(angles), jnp.sin(angles))


def rotate(values, cosines, sine_vals):
    half_size = values.shape[-1] // 2
    first_half = values[..., :half_size]
    second_half = values[..., half_size:]
    return jnp.concatenate(
        [
            first_half * cosines - second_half * sine_vals,
            second_half * cosines + first_half * sine_vals,
        ],
        axis=-1,
    )


def add_branch(branch, base_rows, gain_vec):
    return base_rows + rms_scale(branch, gain_vec)


def activate(gate_up):
    return gelu_tanh(gate_up[:, :FF]) * gate_up[:, FF:]


def body(tokens, w_qkv, w_out, w_gate_up, w_down, norm_gains, block_order, cotangent):
    seq_count, tok_rows, _ = tokens.shape
    block_len = tok_rows // 2
    ctx_size = lax.axis_size("ctx")
    ctx_index = lax.axis_index("ctx")
    score_scale = HD ** (-0.5)
    ctx_parts = (
        lax.all_gather(w_qkv, "ctx", axis=0, tiled=True),
        lax.all_gather(w_out, "ctx", axis=1, tiled=True),
        lax.all_gather(w_gate_up, "ctx", axis=0, tiled=True),
        lax.all_gather(w_down, "ctx", axis=1, tiled=True),
        lax.all_gather(norm_gains, "ctx", axis=0, tiled=True),
    )
    part_qkv, part_out, part_gu, part_down, part_gains = ctx_parts
    full_qkv, full_out, full_gu, full_down, full_gains = (
        lax.all_gather(part_qkv, "batch", axis=1, tiled=True),
        lax.all_gather(part_out, "batch", axis=0, tiled=True),
        lax.all_gather(part_gu, "batch", axis=1, tiled=True),
        lax.all_gather(part_down, "batch", axis=0, tiled=True),
        lax.all_gather(part_gains, "batch", axis=0, tiled=True),
    )
    gain_all = full_gains.astype(jnp.float32)
    gain_in = gain_all[0:D]
    gain_attn = gain_all[D : 2 * D]
    gain_pre = gain_all[2 * D : 3 * D]
    gain_post = gain_all[3 * D : 4 * D]
    gain_query = gain_all[4 * D : 4 * D + HD]
    gain_key = gain_all[4 * D + HD : 4 * D + 2 * HD]
    offsets = jnp.arange(block_len, dtype=jnp.int32)
    key_pos = (block_order[:, None] * block_len + offsets[None, :]).reshape(-1)
    query_pos = lax.dynamic_slice_in_dim(key_pos, ctx_index * tok_rows, tok_rows)
    cosines, sine_vals = rope_tables(query_pos, HD)
    flat = tokens.reshape(seq_count * tok_rows, D).astype(jnp.float32)
    normed, back_one = jax.vjp(rms_scale, flat, gain_in)
    normed_b = normed.astype(jnp.bfloat16)
    projected = jnp.dot(normed_b, full_qkv, preferred_element_type=jnp.float32)

    def prepare(raw_proj, gain_q, gain_k):
        shaped = raw_proj.reshape(seq_count, tok_rows, H + 2, HD)
        queries = rotate(
            rms_scale(shaped[:, :, :H], gain_q),
            cosines[None, :, None, :],
            sine_vals[None, :, None, :],
        )
        key_vecs = rotate(rms_scale(shaped[:, :, H], gain_k), cosines[None], sine_vals[None])
        return (queries.transpose(0, 2, 1, 3), key_vecs, shaped[:, :, H + 1])

    (queries, key_vecs, val_vecs), back_prep = jax.vjp(prepare, projected, gain_query, gain_key)
    query_b = queries.astype(jnp.bfloat16)
    key_b = key_vecs.astype(jnp.bfloat16)
    value_b = val_vecs.astype(jnp.bfloat16)

    def scores_for(key_piece, piece_pos):
        allowed = piece_pos[None, :] <= query_pos[:, None]
        raw_scores = (
            jnp.einsum("shrd,snd->shrn", query_b, key_piece, preferred_element_type=jnp.float32)
            * score_scale
        )
        return (jnp.where(allowed, raw_scores, neg_large), allowed)

    stat_shape = (seq_count, H, tok_rows)
    row_max = jnp.full(stat_shape, neg_large, jnp.float32)
    key_piece = lax.all_gather(key_b, "ctx", axis=1, tiled=True)
    value_piece = lax.all_gather(value_b, "ctx", axis=1, tiled=True)
    piece_pos = key_pos
    scores, allowed = scores_for(key_piece, piece_pos)
    new_max = jnp.maximum(row_max, jnp.max(scores, axis=-1))
    powers = jnp.where(allowed, jnp.exp(scores - new_max[..., None]), 0.0)
    row_total = jnp.sum(powers, axis=-1)
    weighted = jnp.einsum(
        "shrn,snd->shrd",
        powers.astype(jnp.bfloat16),
        value_piece,
        preferred_element_type=jnp.float32,
    )
    row_max, row_total, weighted = (new_max, row_total, weighted)
    attn_out = weighted / row_total[..., None]
    log_total = row_max + jnp.log(row_total)
    attn_b = (
        attn_out.transpose(0, 2, 1, 3).reshape(seq_count * tok_rows, H * HD).astype(jnp.bfloat16)
    )
    y_attn = jnp.dot(attn_b, full_out, preferred_element_type=jnp.float32)
    residual, back_attn = jax.vjp(add_branch, y_attn, flat, gain_attn)
    normed_two, back_two = jax.vjp(rms_scale, residual, gain_pre)
    normed_two_b = normed_two.astype(jnp.bfloat16)
    gate_up = jnp.dot(normed_two_b, full_gu, preferred_element_type=jnp.float32)
    hidden, back_act = jax.vjp(activate, gate_up)
    hidden_b = hidden.astype(jnp.bfloat16)
    branch = jnp.dot(hidden_b, full_down, preferred_element_type=jnp.float32)
    output, back_out = jax.vjp(add_branch, branch, residual, gain_post)
    result = output.astype(jnp.bfloat16).reshape(tokens.shape)
    seed_grad = cotangent.reshape(seq_count * tok_rows, D).astype(jnp.float32)
    d_branch, d_resid_a, d_gain_post = back_out(seed_grad)
    d_branch_b = d_branch.astype(jnp.bfloat16)
    grad_down = jnp.einsum("tf,td->fd", hidden_b, d_branch_b, preferred_element_type=jnp.float32)
    d_hidden = jnp.einsum("td,fd->tf", d_branch_b, full_down, preferred_element_type=jnp.float32)
    (d_gate_up,) = back_act(d_hidden)
    d_gate_up_b = d_gate_up.astype(jnp.bfloat16)
    grad_gu = jnp.einsum("td,tf->df", normed_two_b, d_gate_up_b, preferred_element_type=jnp.float32)
    d_normed_two = jnp.einsum("tf,df->td", d_gate_up_b, full_gu, preferred_element_type=jnp.float32)
    d_resid_b, d_gain_pre = back_two(d_normed_two)
    d_y_attn, d_flat_a, d_gain_attn = back_attn(d_resid_a + d_resid_b)
    d_y_attn_b = d_y_attn.astype(jnp.bfloat16)
    grad_out = jnp.einsum("te,td->ed", attn_b, d_y_attn_b, preferred_element_type=jnp.float32)
    d_attn_rows = jnp.einsum(
        "td,ed->te", d_y_attn_b, full_out, preferred_element_type=jnp.float32
    ).astype(jnp.bfloat16)
    d_attn = d_attn_rows.reshape(seq_count, tok_rows, H, HD).transpose(0, 2, 1, 3)
    row_dot = jnp.sum(d_attn.astype(jnp.float32) * attn_out, axis=-1)

    def piece_grads(key_piece, value_piece, piece_pos):
        scores, allowed = scores_for(key_piece, piece_pos)
        soft_probs = jnp.where(allowed, jnp.exp(scores - log_total[..., None]), 0.0)
        d_probs = jnp.einsum(
            "shrd,snd->shrn", d_attn, value_piece, preferred_element_type=jnp.float32
        )
        d_scores = (soft_probs * (d_probs - row_dot[..., None])).astype(jnp.bfloat16)
        d_query = (
            jnp.einsum("shrn,snd->shrd", d_scores, key_piece, preferred_element_type=jnp.float32)
            * score_scale
        )
        d_key = (
            jnp.einsum("shrn,shrd->snd", d_scores, query_b, preferred_element_type=jnp.float32)
            * score_scale
        )
        d_value = jnp.einsum(
            "shrn,shrd->snd",
            soft_probs.astype(jnp.bfloat16),
            d_attn,
            preferred_element_type=jnp.float32,
        )
        return (d_query, d_key, d_value)

    def cycle_turn(turn_index, loop_state):
        key_piece, value_piece, sum_key, sum_value, sum_query = loop_state
        owner_index = (ctx_index - turn_index) % ctx_size
        piece_pos = lax.dynamic_slice_in_dim(key_pos, owner_index * tok_rows, tok_rows)
        d_query, d_key, d_value = piece_grads(key_piece, value_piece, piece_pos)
        key_piece, value_piece = passed_along((key_piece, value_piece), "ctx", 1)
        sum_key, sum_value = (
            passed_along((sum_key + d_key).astype(jnp.bfloat16), "ctx", 1).astype(jnp.float32),
            passed_along((sum_value + d_value).astype(jnp.bfloat16), "ctx", 1).astype(jnp.float32),
        )
        return (key_piece, value_piece, sum_key, sum_value, sum_query + d_query)

    zero_kv = jnp.zeros(key_b.shape, jnp.float32)
    final_state = lax.fori_loop(
        0,
        ctx_size,
        cycle_turn,
        (key_b, value_b, zero_kv, zero_kv, jnp.zeros(query_b.shape, jnp.float32)),
    )
    grad_key = final_state[2]
    grad_value = final_state[3]
    grad_query = final_state[4]
    d_projected, d_gain_query, d_gain_key = back_prep((grad_query, grad_key, grad_value))
    d_projected_b = d_projected.astype(jnp.bfloat16)
    grad_qkv = jnp.einsum("td,te->de", normed_b, d_projected_b, preferred_element_type=jnp.float32)
    d_normed = jnp.einsum("te,de->td", d_projected_b, full_qkv, preferred_element_type=jnp.float32)
    d_flat_b, d_gain_in = back_one(d_normed)
    grad_tokens = (d_flat_a + d_flat_b).reshape(tokens.shape)
    grad_gain_all = jnp.concatenate(
        [d_gain_in, d_gain_attn, d_gain_pre, d_gain_post, d_gain_query, d_gain_key]
    )
    batch_sums = (
        lax.psum_scatter(
            grad_qkv.astype(jnp.bfloat16), "batch", scatter_dimension=1, tiled=True
        ).astype(jnp.float32),
        lax.psum_scatter(
            grad_out.astype(jnp.bfloat16), "batch", scatter_dimension=0, tiled=True
        ).astype(jnp.float32),
        lax.psum_scatter(
            grad_gu.astype(jnp.bfloat16), "batch", scatter_dimension=1, tiled=True
        ).astype(jnp.float32),
        lax.psum_scatter(
            grad_down.astype(jnp.bfloat16), "batch", scatter_dimension=0, tiled=True
        ).astype(jnp.float32),
        lax.psum_scatter(
            grad_gain_all.astype(jnp.bfloat16), "batch", scatter_dimension=0, tiled=True
        ).astype(jnp.float32),
    )
    sum_qkv, sum_out, sum_gu, sum_down, sum_gains = batch_sums
    final_qkv, final_out, final_gu, final_down, final_gains = (
        lax.psum_scatter(
            sum_qkv.astype(jnp.bfloat16), "ctx", scatter_dimension=0, tiled=True
        ).astype(jnp.float32),
        lax.psum_scatter(
            sum_out.astype(jnp.bfloat16), "ctx", scatter_dimension=1, tiled=True
        ).astype(jnp.float32),
        lax.psum_scatter(
            sum_gu.astype(jnp.bfloat16), "ctx", scatter_dimension=0, tiled=True
        ).astype(jnp.float32),
        lax.psum_scatter(
            sum_down.astype(jnp.bfloat16), "ctx", scatter_dimension=1, tiled=True
        ).astype(jnp.float32),
        lax.psum_scatter(
            sum_gains.astype(jnp.bfloat16), "ctx", scatter_dimension=0, tiled=True
        ).astype(jnp.float32),
    )
    return (result, grad_tokens, final_qkv, final_out, final_gu, final_down, final_gains)


def solution(mesh):
    in_specs = (
        P("batch", "ctx", None),
        P("ctx", "batch"),
        P("batch", "ctx"),
        P("ctx", "batch"),
        P("batch", "ctx"),
        P(("batch", "ctx")),
        P(),
        P("batch", "ctx", None),
    )
    out_specs = (
        P("batch", "ctx", None),
        P("batch", "ctx", None),
        P("ctx", "batch"),
        P("batch", "ctx"),
        P("ctx", "batch"),
        P("batch", "ctx"),
        P(("batch", "ctx")),
    )
    return jax.shard_map(body, mesh=mesh, in_specs=in_specs, out_specs=out_specs, check_vma=False)
```

profile of v0, /device:TPU:0, one launch (start us, length us, event | category | flops | bytes accessed | tf_op | source)
XLA Modules:
  0.0 769.5 jit_solution(7192679817751129525)
XLA Ops:
  7.2 17.8 %all_gather.38 = bf16[640,384]{1,0:T(8,128)(2,1)} all-gather(bf16[80,384]{1,0:T(8,128)(2,1)} %param.11), channel_id=1, replica_groups=mesh['batch'=4,'ctx'=8] {'ctx'}, dimensions={0}, use_global_device_ids=true | all-gather | bytes 552960 | tf_op jit(solution)/shard_map/all_gather | solution.py:72
  31.5 17.0 %all-reduce.9 = bf16[768]{0:T(1024)(128)(2,1)S(1)} all-reduce(bf16[768]{0:T(1024)(128)(2,1)S(1)} %dynamic-update-slice), channel_id=1, replica_groups=mesh['batch'=4,'ctx'=8] {'ctx'}, use_global_device_ids=true, to_apply=%add.9 | all-reduce | flops 768 | bytes 3072
  48.4 8.3 %all-gather.1 = bf16[4,1,768]{2,1,0:T(2,128)(2,1)S(1)} all-gather(bf16[1,1,768]{2,1,0:T(2,128)(2,1)S(1)} %reshape.329), channel_id=1, replica_groups=mesh['batch'=4,'ctx'=8] {'batch'}, dimensions={0}, use_global_device_ids=true | all-gather | bytes 7680 | tf_op jit(solution)/shard_map/all_gather | solution.py:84
  60.6 4.0 copy.38
  64.5 3.2 fusion.49
  70.3 16.8 %all_gather.42 = bf16[256,640]{0,1:T(8,128)(2,1)} all-gather(bf16[256,80]{0,1:T(8,128)(2,1)} %param.12), channel_id=1, replica_groups=mesh['batch'=4,'ctx'=8] {'ctx'}, dimensions={1}, use_global_device_ids=true | all-gather | bytes 368640 | tf_op jit(solution)/shard_map/all_gather | solution.py:73
  87.9 17.3 %all_gather.46 = bf16[512,640]{0,1:T(8,128)(2,1)} all-gather(bf16[512,80]{0,1:T(8,128)(2,1)} %param.14), channel_id=1, replica_groups=mesh['batch'=4,'ctx'=8] {'ctx'}, dimensions={1}, use_global_device_ids=true | all-gather | bytes 737280 | tf_op jit(solution)/shard_map/all_gather | solution.py:75
  107.7 13.0 %all-gather.12.cloned.1.call-done = bf16[4,1024,256]{2,1,0:T(8,128)(2,1)} async-done(((bf16[4,128,256]{2,1,0:T(8,128)(2,1)}), bf16[4,1024,256]{2,1,0:T(8,128)(2,1)}) %all-gather.12.cloned.1.call-update) | async-done | bytes 2097168 | tf_op jit(solution)/shard_map/all_gather | solution.py:127
  120.7 3.2 fusion.15
  123.9 3.3 copy-done.18
  127.2 2.8 fusion.16
  130.0 20.9 %all-gather.22.cloned.1.call-done = bf16[4,1024,1,256]{3,1,2,0:T(8,128)(2,1)} async-done(((bf16[4,128,1,256]{3,1,2,0:T(8,128)(2,1)}), bf16[4,1024,1,256]{3,1,2,0:T(8,128)(2,1)}) %all-gather.22.cloned.1.call-update) | async-done | bytes 2097168 | tf_op jit(solution)/shard_map/all_gather | solution.py:128
  150.9 7.3 fusion.29
  159.3 21.5 %all-gather.14.cloned.1.call-done = bf16[1024,640]{0,1:T(8,128)(2,1)} async-done(((bf16[256,640]{0,1:T(8,128)(2,1)}), bf16[1024,640]{0,1:T(8,128)(2,1)}) %all-gather.14.cloned.1.call-update) | async-done | bytes 1310736 | tf_op jit(solution)/shard_map/all_gather | solution.py:81
  180.8 2.5 multiply_reduce_fusion.10
  185.5 58.5 %all-gather.18.cloned.1.call-done = bf16[640,4096]{1,0:T(8,128)(2,1)} async-done(((bf16[640,1024]{1,0:T(8,128)(2,1)}), bf16[640,4096]{1,0:T(8,128)(2,1)}) %all-gather.18.cloned.1.call-update) | async-done | bytes 5242896 | tf_op jit(solution)/shard_map/all_gather | solution.py:82
  243.9 5.5 fusion.65
  249.4 3.3 copy-done.2
  252.7 2.4 multiply_convert_fusion
  255.1 30.1 %all-gather.20.cloned.1.call-done = bf16[2048,640]{0,1:T(8,128)(2,1)} async-done(((bf16[512,640]{0,1:T(8,128)(2,1)}), bf16[2048,640]{0,1:T(8,128)(2,1)}) %all-gather.20.cloned.1.call-update) | async-done | bytes 2621456 | tf_op jit(solution)/shard_map/all_gather | solution.py:83
  285.3 4.4 multiply_reduce_fusion.8
  292.3 18.4 %fusion.35 = (f32[512,2048]{1,0:T(8,128)S(1)}, f32[512,2048]{1,0:T(8,128)S(1)}) fusion(f32[512,4096]{1,0:T(8,128)S(1)} %copy-done.3, bf16[512,640]{1,0:T(8,128)(2,1)S(1)} %get-tuple-element.472, bf16[2048,640]{0,1:T(8,128)(2,1)S(1)} %copy-done.54), kind=kOutput, calls=%fused_computation.71 | convolution fusion | flops 1369440256 | bytes 20054016 | tf_op jit(solution)/shard_map/td,fd->tf/dot_general | solution.py:160
  310.8 4.1 multiply_reduce_fusion.4
  318.0 2.2 convolution_convert_fusion.3
  320.2 2.3 convolution_convert_fusion.4
  326.4 148.2 %while.24 = (s32[]{:T(128)}, bf16[4,128,256]{2,1,0:T(8,128)(2,1)S(1)}, bf16[4,128,256]{2,1,0:T(8,128)(2,1)}, f32[4,128,256]{2,1,0:T(8,128)}, f32[4,128,256]{2,1,...) while((s32[]{:T(128)}, ...), condition=%wide.region_13.14_spmd.clone, body=%wide.region_12.13_spmd.clone.sunk | while | flops 675954688 | bytes 26528312 | solution.py:211
  336.5 1.8 select_add_fusion.2
  338.3 3.5 collective-permute-done.2
  341.8 1.8 convert_element_type.282
  344.6 1.8 convert_element_type.283
  354.6 3.4 select_add_fusion.2
  358.0 2.1 collective-permute-done.2
  360.1 1.8 convert_element_type.282
  372.5 3.4 select_add_fusion.2
  375.9 2.6 collective-permute-done.2
  378.4 1.8 convert_element_type.282
  391.7 3.4 select_add_fusion.2
  396.8 1.8 convert_element_type.282
  410.0 3.4 select_add_fusion.2
  415.1 1.8 convert_element_type.282
  428.3 3.4 select_add_fusion.2
  433.4 1.8 convert_element_type.282
  446.7 3.4 select_add_fusion.2
  451.7 1.8 convert_element_type.282
  465.0 3.4 select_add_fusion.2
  470.1 1.8 convert_element_type.282
  474.7 1.9 copy.89
  483.4 3.6 convolution_convert_fusion.2
  487.1 4.1 copy.57
  491.3 3.3 convolution_convert_fusion.1
  495.9 9.1 %convolution_convert_fusion = bf16[640,4096]{1,0:T(8,128)(2,1)} fusion(f32[512,2048]{1,0:T(8,128)} %copy-done.21, f32[512,2048]{1,0:T(8,128)} %copy-done.20, f32[512,640]{1,0:T(8,128)S(1)} %copy-done.5, f32[640]{0:T(1024)S(1)} %get-tuple-element.479, f32[512]{0:T(512)S(1)} %fusion.56), kind=kOutput, calls=%fused_computation.25 | convolution fusion | flops 2692153344 | bytes 14946816 | tf_op jit(solution)/shard_map/td,tf->df/dot_general | solution.py:163
  505.1 1.9 copy.59
  507.1 17.2 %reduce-scatter.25.cloned.1.call-done = bf16[384,640]{1,0:T(8,128)(2,1)} async-done(((bf16[1536,640]{1,0:T(8,128)(2,1)}), bf16[384,640]{1,0:T(8,128)(2,1)}) %reduce-scatter.25.cloned.1.call-update) | async-done | bytes 491536
  524.3 2.1 copy.58
  526.6 40.1 %reduce-scatter.23.cloned.1.call-done = bf16[512,640]{1,0:T(8,128)(2,1)} async-done(((bf16[2048,640]{1,0:T(8,128)(2,1)}), bf16[512,640]{1,0:T(8,128)(2,1)}) %reduce-scatter.23.cloned.1.call-update) | async-done | bytes 655376 | tf_op jit(solution)/shard_map/reduce_scatter | solution.py:239
  566.7 2.2 copy.61
  569.0 62.2 %reduce-scatter.19.cloned.1.call-done = bf16[640,1024]{1,0:T(8,128)(2,1)} async-done(((bf16[640,4096]{1,0:T(8,128)(2,1)}), bf16[640,1024]{1,0:T(8,128)(2,1)}) %reduce-scatter.19.cloned.1.call-update) | async-done | bytes 1310736 | tf_op jit(solution)/shard_map/reduce_scatter | solution.py:236
  633.2 4.9 fusion.48
  646.4 9.2 %all-reduce.10 = bf16[3072]{0:T(1024)(128)(2,1)S(1)} all-reduce(bf16[3072]{0:T(1024)(128)(2,1)} %dynamic-update-slice.6), channel_id=11, replica_groups=mesh['batch'=4,'ctx'=8] {'batch'}, use_global_device_ids=true, to_apply=%region_31.32.clone | all-reduce | flops 3072 | bytes 12288
  655.7 14.3 %all-reduce.11 = bf16[768]{0:T(1024)(128)(2,1)S(1)} all-reduce(bf16[768]{0:T(1024)(128)(2,1)S(1)} %dynamic-slice.2), channel_id=12, replica_groups=mesh['batch'=4,'ctx'=8] {'ctx'}, use_global_device_ids=true, to_apply=%region_32.33.clone | all-reduce | flops 768 | bytes 3072
  671.3 2.7 fusion.41
  675.7 20.2 %reduce-scatter.15.cloned.1.call-done = bf16[80,384]{1,0:T(8,128)(2,1)} async-done(((bf16[640,384]{1,0:T(8,128)(2,1)}), bf16[80,384]{1,0:T(8,128)(2,1)}) %reduce-scatter.15.cloned.1.call-update) | async-done | bytes 61456 | tf_op jit(solution)/shard_map/reduce_scatter | solution.py:248
  697.4 30.1 %reduce-scatter.29.cloned.1.call-done = bf16[80,512]{1,0:T(8,128)(2,1)} async-done(((bf16[640,512]{1,0:T(8,128)(2,1)}), bf16[80,512]{1,0:T(8,128)(2,1)}) %reduce-scatter.29.cloned.1.call-update) | async-done | bytes 81936
  729.4 31.7 %reduce-scatter.21.cloned.1.call-done = bf16[80,1024]{1,0:T(8,128)(2,1)} async-done(((bf16[640,1024]{1,0:T(8,128)(2,1)}), bf16[80,1024]{1,0:T(8,128)(2,1)}) %reduce-scatter.21.cloned.1.call-update) | async-done | bytes 163856 | tf_op jit(solution)/shard_map/reduce_scatter | solution.py:254
  (388 shorter events, 151.7 us)
Async XLA Ops:
  7.2 51.0 %copy-start.15 = (bf16[4,128,640]{2,1,0:T(8,128)(2,1)S(1)}, bf16[4,128,640]{2,1,0:T(8,128)(2,1)}, u32[]{:S(2)}) copy-start(bf16[4,128,640]{2,1,0:T(8,128)(2,1)} %param.10) | copy-start | bytes 1966084
  7.2 53.4 %all-gather.10.cloned.1.call-start = ((), (), s32[]{:S(2)}) async-start(), calls=%async_computation.8 | async-start | bytes 2457600 | tf_op jit(solution)/shard_map/all_gather | solution.py:80
  25.1 62.7 %all-gather.16.cloned.1.call-start = ((), (), s32[]{:S(2)}) async-start(), calls=%async_computation.11 | async-start | bytes 1474560 | tf_op jit(solution)/shard_map/all_gather | solution.py:74
  25.8 94.9 %all-gather.12.cloned.1.call-start = ((), (), s32[]{:S(2)}) async-start(), calls=%async_computation.9 | async-start | bytes 2359296 | tf_op jit(solution)/shard_map/all_gather | solution.py:127
  26.7 21.8 %copy-start.45 = (s32[1024]{0:T(1024)}, s32[1024]{0:T(1024)S(1)}, u32[]{:S(2)}) copy-start(s32[1024]{0:T(1024)S(1)} %add.250) | copy-start | bytes 12292
  28.6 76.7 %copy-start.44 = (s32[128]{0:T(128)}, s32[128]{0:T(128)S(1)}, u32[]{:S(2)}) copy-start(s32[128]{0:T(128)S(1)} %get-tuple-element.585) | copy-start | bytes 1540
  57.9 125.4 %copy-start.35 = (f32[640]{0:T(1024)}, f32[640]{0:T(1024)S(1)}, u32[]{:S(2)}) copy-start(f32[640]{0:T(1024)S(1)} %get-tuple-element.480) | copy-start | bytes 7684
  67.7 38.9 %copy-start = (f32[4,128,6,256]{3,1,2,0:T(8,128)}, f32[4,128,6,256]{3,1,2,0:T(8,128)S(1)}, u32[]{:S(2)}) copy-start(f32[4,128,6,256]{3,1,2,0:T(8,128)S(1)} %fusion.49) | copy-start | bytes 9437188
  69.5 35.8 %copy-start.46 = (s32[1024]{0:T(1024)S(1)}, s32[1024]{0:T(1024)}, u32[]{:S(2)}) copy-start(s32[1024]{0:T(1024)} %copy-done.45) | copy-start | bytes 12292
  69.5 81.4 %all-gather.22.cloned.1.call-start = ((), (), s32[]{:S(2)}) async-start(), calls=%async_computation.19 | async-start | bytes 2359296 | tf_op jit(solution)/shard_map/all_gather | solution.py:128
  70.3 110.5 %all-gather.14.cloned.1.call-start = ((), (), s32[]{:S(2)}) async-start(), calls=%async_computation.10 | async-start | bytes 1638400 | tf_op jit(solution)/shard_map/all_gather | solution.py:81
  87.1 156.8 %all-gather.18.cloned.1.call-start = ((), (), s32[]{:S(2)}) async-start(), calls=%async_computation.12 | async-start | bytes 6553600 | tf_op jit(solution)/shard_map/all_gather | solution.py:82
  87.8 197.5 %all-gather.20.cloned.1.call-start = ((), (), s32[]{:S(2)}) async-start(), calls=%async_computation.13 | async-start | bytes 3276800 | tf_op jit(solution)/shard_map/all_gather | solution.py:83
  105.2 399.9 %reduce-scatter.17.cloned.1.call-start = ((), (), s32[]{:S(2)}) async-start(), calls=%async_computation.15 | async-start | bytes 1638400 | tf_op jit(solution)/shard_map/reduce_scatter | solution.py:233
  130.0 54.8 %copy-start.34 = (f32[4,4,128]{2,1,0:T(4,128)}, f32[4,4,128]{2,1,0:T(4,128)S(1)}, u32[]{:S(2)}) copy-start(f32[4,4,128]{2,1,0:T(4,128)S(1)} %fusion.16) | copy-start | bytes 24580
  159.3 24.0 %copy-start.26 = (bf16[64,8,4,256]{3,1,2,0:T(8,128)(2,1)}, bf16[64,8,4,256]{3,1,2,0:T(8,128)(2,1)S(1)}, u32[]{:S(2)}) copy-start(bf16[64,8,4,256]{3,1,2,0:T(8,128)(2,1)S(1)} %copy.64) | copy-start | bytes 3145732
  184.8 130.2 %copy-start.4 = (f32[512,640]{1,0:T(8,128)}, f32[512,640]{1,0:T(8,128)S(1)}, u32[]{:S(2)}) copy-start(f32[512,640]{1,0:T(8,128)S(1)} %get-tuple-element.463) | copy-start | bytes 3932164
  255.1 34.6 %copy-start.19 = (bf16[4,128,640]{2,1,0:T(8,128)(2,1)S(1)}, bf16[4,128,640]{2,1,0:T(8,128)(2,1)}, u32[]{:S(2)}) copy-start(bf16[4,128,640]{2,1,0:T(8,128)(2,1)} %param.17) | copy-start | bytes 1966084
  255.1 34.6 %copy-start.39 = (f32[640]{0:T(1024)S(1)}, f32[640]{0:T(1024)}, u32[]{:S(2)}) copy-start(f32[640]{0:T(1024)} %get-tuple-element.478) | copy-start | bytes 7684
  326.4 197.9 %reduce-scatter.25.cloned.1.call-start = ((), (), s32[]{:S(2)}) async-start(), calls=%async_computation.20 | async-start | bytes 2457600
  326.5 19.9 %collective-permute-start = (bf16[4,128,256]{2,1,0:T(8,128)(2,1)S(1)}, bf16[4,128,256]{2,1,0:T(8,128)(2,1)S(1)}, u32[]{:S(2)}, u32[]{:S(2)}) collective-permute-start(bf16[4,128,256]{2,1,0:T(8,128)(2,1)S(1)} %copy.99), channel_id=1, source_target_pairs={{0,1},{1,2},{2,3},{3,4},{4,5},{5,6},{6,7},{7,0},{8,9},{9,10},{10,1... | collective-permute-start | bytes 786440 | tf_op jit(solution)/shard_map/while/body/eval_jaxpr/ppermute | solution.py:20
  327.5 18.9 %collective-permute-start.1 = (bf16[4,128,256]{2,1,0:T(8,128)(2,1)S(1)}, bf16[4,128,256]{2,1,0:T(8,128)(2,1)}, u32[]{:S(2)}, u32[]{:S(2)}) collective-permute-start(bf16[4,128,256]{2,1,0:T(8,128)(2,1)S(1)} %copy.100), channel_id=1, source_target_pairs={{0,1},{1,2},{2,3},{3,4},{4,5},{5,6},{6,7},{7,0},{8,9},{9,10},{10,1... | collective-permute-start | bytes 786440 | tf_op jit(solution)/shard_map/while/body/eval_jaxpr/ppermute | solution.py:20
  333.8 7.9 %collective-permute-start.2 = (bf16[4,128,256]{2,1,0:T(8,128)(2,1)}, bf16[4,128,256]{2,1,0:T(8,128)(2,1)}, u32[]{:S(2)}, u32[]{:S(2)}) collective-permute-start(bf16[4,128,256]{2,1,0:T(8,128)(2,1)} %fusion.121), channel_id=1, source_target_pairs={{0,1},{1,2},{2,3},{3,4},{4,5},{5,6},{6,7},{7,0},{8,9},{9,10},{10,1... | collective-permute-start | bytes 786440 | tf_op jit(solution)/shard_map/while/body/eval_jaxpr/ppermute | solution.py:20
  334.9 9.6 %collective-permute-start.3 = (bf16[4,128,256]{2,1,0:T(8,128)(2,1)}, bf16[4,128,256]{2,1,0:T(8,128)(2,1)}, u32[]{:S(2)}, u32[]{:S(2)}) collective-permute-start(bf16[4,128,256]{2,1,0:T(8,128)(2,1)} %fusion.122), channel_id=1, source_target_pairs={{0,1},{1,2},{2,3},{3,4},{4,5},{5,6},{6,7},{7,0},{8,9},{9,10},{10,1... | collective-permute-start | bytes 786440 | tf_op jit(solution)/shard_map/while/body/eval_jaxpr/ppermute | solution.py:20
  346.4 18.3 %collective-permute-start = (bf16[4,128,256]{2,1,0:T(8,128)(2,1)S(1)}, bf16[4,128,256]{2,1,0:T(8,128)(2,1)S(1)}, u32[]{:S(2)}, u32[]{:S(2)}) collective-permute-start(bf16[4,128,256]{2,1,0:T(8,128)(2,1)S(1)} %copy.99), channel_id=1, source_target_pairs={{0,1},{1,2},{2,3},{3,4},{4,5},{5,6},{6,7},{7,0},{8,9},{9,10},{10,1... | collective-permute-start | bytes 786440 | tf_op jit(solution)/shard_map/while/body/eval_jaxpr/ppermute | solution.py:20
  347.4 17.3 %collective-permute-start.1 = (bf16[4,128,256]{2,1,0:T(8,128)(2,1)S(1)}, bf16[4,128,256]{2,1,0:T(8,128)(2,1)}, u32[]{:S(2)}, u32[]{:S(2)}) collective-permute-start(bf16[4,128,256]{2,1,0:T(8,128)(2,1)S(1)} %copy.100), channel_id=1, source_target_pairs={{0,1},{1,2},{2,3},{3,4},{4,5},{5,6},{6,7},{7,0},{8,9},{9,10},{10,1... | collective-permute-start | bytes 786440 | tf_op jit(solution)/shard_map/while/body/eval_jaxpr/ppermute | solution.py:20
  352.2 7.9 %collective-permute-start.2 = (bf16[4,128,256]{2,1,0:T(8,128)(2,1)}, bf16[4,128,256]{2,1,0:T(8,128)(2,1)}, u32[]{:S(2)}, u32[]{:S(2)}) collective-permute-start(bf16[4,128,256]{2,1,0:T(8,128)(2,1)} %fusion.121), channel_id=1, source_target_pairs={{0,1},{1,2},{2,3},{3,4},{4,5},{5,6},{6,7},{7,0},{8,9},{9,10},{10,1... | collective-permute-start | bytes 786440 | tf_op jit(solution)/shard_map/while/body/eval_jaxpr/ppermute | solution.py:20
  353.2 9.7 %collective-permute-start.3 = (bf16[4,128,256]{2,1,0:T(8,128)(2,1)}, bf16[4,128,256]{2,1,0:T(8,128)(2,1)}, u32[]{:S(2)}, u32[]{:S(2)}) collective-permute-start(bf16[4,128,256]{2,1,0:T(8,128)(2,1)} %fusion.122), channel_id=1, source_target_pairs={{0,1},{1,2},{2,3},{3,4},{4,5},{5,6},{6,7},{7,0},{8,9},{9,10},{10,1... | collective-permute-start | bytes 786440 | tf_op jit(solution)/shard_map/while/body/eval_jaxpr/ppermute | solution.py:20
  364.7 18.3 %collective-permute-start = (bf16[4,128,256]{2,1,0:T(8,128)(2,1)S(1)}, bf16[4,128,256]{2,1,0:T(8,128)(2,1)S(1)}, u32[]{:S(2)}, u32[]{:S(2)}) collective-permute-start(bf16[4,128,256]{2,1,0:T(8,128)(2,1)S(1)} %copy.99), channel_id=1, source_target_pairs={{0,1},{1,2},{2,3},{3,4},{4,5},{5,6},{6,7},{7,0},{8,9},{9,10},{10,1... | collective-permute-start | bytes 786440 | tf_op jit(solution)/shard_map/while/body/eval_jaxpr/ppermute | solution.py:20
  365.7 17.3 %collective-permute-start.1 = (bf16[4,128,256]{2,1,0:T(8,128)(2,1)S(1)}, bf16[4,128,256]{2,1,0:T(8,128)(2,1)}, u32[]{:S(2)}, u32[]{:S(2)}) collective-permute-start(bf16[4,128,256]{2,1,0:T(8,128)(2,1)S(1)} %copy.100), channel_id=1, source_target_pairs={{0,1},{1,2},{2,3},{3,4},{4,5},{5,6},{6,7},{7,0},{8,9},{9,10},{10,1... | collective-permute-start | bytes 786440 | tf_op jit(solution)/shard_map/while/body/eval_jaxpr/ppermute | solution.py:20
  370.5 7.9 %collective-permute-start.2 = (bf16[4,128,256]{2,1,0:T(8,128)(2,1)}, bf16[4,128,256]{2,1,0:T(8,128)(2,1)}, u32[]{:S(2)}, u32[]{:S(2)}) collective-permute-start(bf16[4,128,256]{2,1,0:T(8,128)(2,1)} %fusion.121), channel_id=1, source_target_pairs={{0,1},{1,2},{2,3},{3,4},{4,5},{5,6},{6,7},{7,0},{8,9},{9,10},{10,1... | collective-permute-start | bytes 786440 | tf_op jit(solution)/shard_map/while/body/eval_jaxpr/ppermute | solution.py:20
  371.6 9.7 %collective-permute-start.3 = (bf16[4,128,256]{2,1,0:T(8,128)(2,1)}, bf16[4,128,256]{2,1,0:T(8,128)(2,1)}, u32[]{:S(2)}, u32[]{:S(2)}) collective-permute-start(bf16[4,128,256]{2,1,0:T(8,128)(2,1)} %fusion.122), channel_id=1, source_target_pairs={{0,1},{1,2},{2,3},{3,4},{4,5},{5,6},{6,7},{7,0},{8,9},{9,10},{10,1... | collective-permute-start | bytes 786440 | tf_op jit(solution)/shard_map/while/body/eval_jaxpr/ppermute | solution.py:20
  383.0 18.3 %collective-permute-start = (bf16[4,128,256]{2,1,0:T(8,128)(2,1)S(1)}, bf16[4,128,256]{2,1,0:T(8,128)(2,1)S(1)}, u32[]{:S(2)}, u32[]{:S(2)}) collective-permute-start(bf16[4,128,256]{2,1,0:T(8,128)(2,1)S(1)} %copy.99), channel_id=1, source_target_pairs={{0,1},{1,2},{2,3},{3,4},{4,5},{5,6},{6,7},{7,0},{8,9},{9,10},{10,1... | collective-permute-start | bytes 786440 | tf_op jit(solution)/shard_map/while/body/eval_jaxpr/ppermute | solution.py:20
  384.0 17.3 %collective-permute-start.1 = (bf16[4,128,256]{2,1,0:T(8,128)(2,1)S(1)}, bf16[4,128,256]{2,1,0:T(8,128)(2,1)}, u32[]{:S(2)}, u32[]{:S(2)}) collective-permute-start(bf16[4,128,256]{2,1,0:T(8,128)(2,1)S(1)} %copy.100), channel_id=1, source_target_pairs={{0,1},{1,2},{2,3},{3,4},{4,5},{5,6},{6,7},{7,0},{8,9},{9,10},{10,1... | collective-permute-start | bytes 786440 | tf_op jit(solution)/shard_map/while/body/eval_jaxpr/ppermute | solution.py:20
  388.8 7.9 %collective-permute-start.2 = (bf16[4,128,256]{2,1,0:T(8,128)(2,1)}, bf16[4,128,256]{2,1,0:T(8,128)(2,1)}, u32[]{:S(2)}, u32[]{:S(2)}) collective-permute-start(bf16[4,128,256]{2,1,0:T(8,128)(2,1)} %fusion.121), channel_id=1, source_target_pairs={{0,1},{1,2},{2,3},{3,4},{4,5},{5,6},{6,7},{7,0},{8,9},{9,10},{10,1... | collective-permute-start | bytes 786440 | tf_op jit(solution)/shard_map/while/body/eval_jaxpr/ppermute | solution.py:20
  389.9 9.7 %collective-permute-start.3 = (bf16[4,128,256]{2,1,0:T(8,128)(2,1)}, bf16[4,128,256]{2,1,0:T(8,128)(2,1)}, u32[]{:S(2)}, u32[]{:S(2)}) collective-permute-start(bf16[4,128,256]{2,1,0:T(8,128)(2,1)} %fusion.122), channel_id=1, source_target_pairs={{0,1},{1,2},{2,3},{3,4},{4,5},{5,6},{6,7},{7,0},{8,9},{9,10},{10,1... | collective-permute-start | bytes 786440 | tf_op jit(solution)/shard_map/while/body/eval_jaxpr/ppermute | solution.py:20
  401.4 18.3 %collective-permute-start = (bf16[4,128,256]{2,1,0:T(8,128)(2,1)S(1)}, bf16[4,128,256]{2,1,0:T(8,128)(2,1)S(1)}, u32[]{:S(2)}, u32[]{:S(2)}) collective-permute-start(bf16[4,128,256]{2,1,0:T(8,128)(2,1)S(1)} %copy.99), channel_id=1, source_target_pairs={{0,1},{1,2},{2,3},{3,4},{4,5},{5,6},{6,7},{7,0},{8,9},{9,10},{10,1... | collective-permute-start | bytes 786440 | tf_op jit(solution)/shard_map/while/body/eval_jaxpr/ppermute | solution.py:20
  402.4 17.3 %collective-permute-start.1 = (bf16[4,128,256]{2,1,0:T(8,128)(2,1)S(1)}, bf16[4,128,256]{2,1,0:T(8,128)(2,1)}, u32[]{:S(2)}, u32[]{:S(2)}) collective-permute-start(bf16[4,128,256]{2,1,0:T(8,128)(2,1)S(1)} %copy.100), channel_id=1, source_target_pairs={{0,1},{1,2},{2,3},{3,4},{4,5},{5,6},{6,7},{7,0},{8,9},{9,10},{10,1... | collective-permute-start | bytes 786440 | tf_op jit(solution)/shard_map/while/body/eval_jaxpr/ppermute | solution.py:20
  407.2 7.9 %collective-permute-start.2 = (bf16[4,128,256]{2,1,0:T(8,128)(2,1)}, bf16[4,128,256]{2,1,0:T(8,128)(2,1)}, u32[]{:S(2)}, u32[]{:S(2)}) collective-permute-start(bf16[4,128,256]{2,1,0:T(8,128)(2,1)} %fusion.121), channel_id=1, source_target_pairs={{0,1},{1,2},{2,3},{3,4},{4,5},{5,6},{6,7},{7,0},{8,9},{9,10},{10,1... | collective-permute-start | bytes 786440 | tf_op jit(solution)/shard_map/while/body/eval_jaxpr/ppermute | solution.py:20
  408.2 9.7 %collective-permute-start.3 = (bf16[4,128,256]{2,1,0:T(8,128)(2,1)}, bf16[4,128,256]{2,1,0:T(8,128)(2,1)}, u32[]{:S(2)}, u32[]{:S(2)}) collective-permute-start(bf16[4,128,256]{2,1,0:T(8,128)(2,1)} %fusion.122), channel_id=1, source_target_pairs={{0,1},{1,2},{2,3},{3,4},{4,5},{5,6},{6,7},{7,0},{8,9},{9,10},{10,1... | collective-permute-start | bytes 786440 | tf_op jit(solution)/shard_map/while/body/eval_jaxpr/ppermute | solution.py:20
  419.7 18.3 %collective-permute-start = (bf16[4,128,256]{2,1,0:T(8,128)(2,1)S(1)}, bf16[4,128,256]{2,1,0:T(8,128)(2,1)S(1)}, u32[]{:S(2)}, u32[]{:S(2)}) collective-permute-start(bf16[4,128,256]{2,1,0:T(8,128)(2,1)S(1)} %copy.99), channel_id=1, source_target_pairs={{0,1},{1,2},{2,3},{3,4},{4,5},{5,6},{6,7},{7,0},{8,9},{9,10},{10,1... | collective-permute-start | bytes 786440 | tf_op jit(solution)/shard_map/while/body/eval_jaxpr/ppermute | solution.py:20
  420.7 17.3 %collective-permute-start.1 = (bf16[4,128,256]{2,1,0:T(8,128)(2,1)S(1)}, bf16[4,128,256]{2,1,0:T(8,128)(2,1)}, u32[]{:S(2)}, u32[]{:S(2)}) collective-permute-start(bf16[4,128,256]{2,1,0:T(8,128)(2,1)S(1)} %copy.100), channel_id=1, source_target_pairs={{0,1},{1,2},{2,3},{3,4},{4,5},{5,6},{6,7},{7,0},{8,9},{9,10},{10,1... | collective-permute-start | bytes 786440 | tf_op jit(solution)/shard_map/while/body/eval_jaxpr/ppermute | solution.py:20
  425.5 7.9 %collective-permute-start.2 = (bf16[4,128,256]{2,1,0:T(8,128)(2,1)}, bf16[4,128,256]{2,1,0:T(8,128)(2,1)}, u32[]{:S(2)}, u32[]{:S(2)}) collective-permute-start(bf16[4,128,256]{2,1,0:T(8,128)(2,1)} %fusion.121), channel_id=1, source_target_pairs={{0,1},{1,2},{2,3},{3,4},{4,5},{5,6},{6,7},{7,0},{8,9},{9,10},{10,1... | collective-permute-start | bytes 786440 | tf_op jit(solution)/shard_map/while/body/eval_jaxpr/ppermute | solution.py:20
  426.6 9.7 %collective-permute-start.3 = (bf16[4,128,256]{2,1,0:T(8,128)(2,1)}, bf16[4,128,256]{2,1,0:T(8,128)(2,1)}, u32[]{:S(2)}, u32[]{:S(2)}) collective-permute-start(bf16[4,128,256]{2,1,0:T(8,128)(2,1)} %fusion.122), channel_id=1, source_target_pairs={{0,1},{1,2},{2,3},{3,4},{4,5},{5,6},{6,7},{7,0},{8,9},{9,10},{10,1... | collective-permute-start | bytes 786440 | tf_op jit(solution)/shard_map/while/body/eval_jaxpr/ppermute | solution.py:20
  438.0 18.3 %collective-permute-start = (bf16[4,128,256]{2,1,0:T(8,128)(2,1)S(1)}, bf16[4,128,256]{2,1,0:T(8,128)(2,1)S(1)}, u32[]{:S(2)}, u32[]{:S(2)}) collective-permute-start(bf16[4,128,256]{2,1,0:T(8,128)(2,1)S(1)} %copy.99), channel_id=1, source_target_pairs={{0,1},{1,2},{2,3},{3,4},{4,5},{5,6},{6,7},{7,0},{8,9},{9,10},{10,1... | collective-permute-start | bytes 786440 | tf_op jit(solution)/shard_map/while/body/eval_jaxpr/ppermute | solution.py:20
  439.0 17.3 %collective-permute-start.1 = (bf16[4,128,256]{2,1,0:T(8,128)(2,1)S(1)}, bf16[4,128,256]{2,1,0:T(8,128)(2,1)}, u32[]{:S(2)}, u32[]{:S(2)}) collective-permute-start(bf16[4,128,256]{2,1,0:T(8,128)(2,1)S(1)} %copy.100), channel_id=1, source_target_pairs={{0,1},{1,2},{2,3},{3,4},{4,5},{5,6},{6,7},{7,0},{8,9},{9,10},{10,1... | collective-permute-start | bytes 786440 | tf_op jit(solution)/shard_map/while/body/eval_jaxpr/ppermute | solution.py:20
  443.8 7.9 %collective-permute-start.2 = (bf16[4,128,256]{2,1,0:T(8,128)(2,1)}, bf16[4,128,256]{2,1,0:T(8,128)(2,1)}, u32[]{:S(2)}, u32[]{:S(2)}) collective-permute-start(bf16[4,128,256]{2,1,0:T(8,128)(2,1)} %fusion.121), channel_id=1, source_target_pairs={{0,1},{1,2},{2,3},{3,4},{4,5},{5,6},{6,7},{7,0},{8,9},{9,10},{10,1... | collective-permute-start | bytes 786440 | tf_op jit(solution)/shard_map/while/body/eval_jaxpr/ppermute | solution.py:20
  444.9 9.7 %collective-permute-start.3 = (bf16[4,128,256]{2,1,0:T(8,128)(2,1)}, bf16[4,128,256]{2,1,0:T(8,128)(2,1)}, u32[]{:S(2)}, u32[]{:S(2)}) collective-permute-start(bf16[4,128,256]{2,1,0:T(8,128)(2,1)} %fusion.122), channel_id=1, source_target_pairs={{0,1},{1,2},{2,3},{3,4},{4,5},{5,6},{6,7},{7,0},{8,9},{9,10},{10,1... | collective-permute-start | bytes 786440 | tf_op jit(solution)/shard_map/while/body/eval_jaxpr/ppermute | solution.py:20
  456.4 18.3 %collective-permute-start = (bf16[4,128,256]{2,1,0:T(8,128)(2,1)S(1)}, bf16[4,128,256]{2,1,0:T(8,128)(2,1)S(1)}, u32[]{:S(2)}, u32[]{:S(2)}) collective-permute-start(bf16[4,128,256]{2,1,0:T(8,128)(2,1)S(1)} %copy.99), channel_id=1, source_target_pairs={{0,1},{1,2},{2,3},{3,4},{4,5},{5,6},{6,7},{7,0},{8,9},{9,10},{10,1... | collective-permute-start | bytes 786440 | tf_op jit(solution)/shard_map/while/body/eval_jaxpr/ppermute | solution.py:20
  457.4 17.3 %collective-permute-start.1 = (bf16[4,128,256]{2,1,0:T(8,128)(2,1)S(1)}, bf16[4,128,256]{2,1,0:T(8,128)(2,1)}, u32[]{:S(2)}, u32[]{:S(2)}) collective-permute-start(bf16[4,128,256]{2,1,0:T(8,128)(2,1)S(1)} %copy.100), channel_id=1, source_target_pairs={{0,1},{1,2},{2,3},{3,4},{4,5},{5,6},{6,7},{7,0},{8,9},{9,10},{10,1... | collective-permute-start | bytes 786440 | tf_op jit(solution)/shard_map/while/body/eval_jaxpr/ppermute | solution.py:20
  462.2 7.9 %collective-permute-start.2 = (bf16[4,128,256]{2,1,0:T(8,128)(2,1)}, bf16[4,128,256]{2,1,0:T(8,128)(2,1)}, u32[]{:S(2)}, u32[]{:S(2)}) collective-permute-start(bf16[4,128,256]{2,1,0:T(8,128)(2,1)} %fusion.121), channel_id=1, source_target_pairs={{0,1},{1,2},{2,3},{3,4},{4,5},{5,6},{6,7},{7,0},{8,9},{9,10},{10,1... | collective-permute-start | bytes 786440 | tf_op jit(solution)/shard_map/while/body/eval_jaxpr/ppermute | solution.py:20
  463.2 9.7 %collective-permute-start.3 = (bf16[4,128,256]{2,1,0:T(8,128)(2,1)}, bf16[4,128,256]{2,1,0:T(8,128)(2,1)}, u32[]{:S(2)}, u32[]{:S(2)}) collective-permute-start(bf16[4,128,256]{2,1,0:T(8,128)(2,1)} %fusion.122), channel_id=1, source_target_pairs={{0,1},{1,2},{2,3},{3,4},{4,5},{5,6},{6,7},{7,0},{8,9},{9,10},{10,1... | collective-permute-start | bytes 786440 | tf_op jit(solution)/shard_map/while/body/eval_jaxpr/ppermute | solution.py:20
  491.2 75.5 %reduce-scatter.23.cloned.1.call-start = ((), (), s32[]{:S(2)}) async-start(), calls=%async_computation.18 | async-start | bytes 3276800 | tf_op jit(solution)/shard_map/reduce_scatter | solution.py:239
  494.6 136.5 %reduce-scatter.19.cloned.1.call-start = ((), (), s32[]{:S(2)}) async-start(), calls=%async_computation.16 | async-start | bytes 6553600 | tf_op jit(solution)/shard_map/reduce_scatter | solution.py:236
  505.0 169.0 %reduce-scatter.27.cloned.1.call-start = ((), (), s32[]{:S(2)}) async-start(), calls=%async_computation.21 | async-start | bytes 368640
  507.0 188.9 %reduce-scatter.15.cloned.1.call-start = ((), (), s32[]{:S(2)}) async-start(), calls=%async_computation.14 | async-start | bytes 552960 | tf_op jit(solution)/shard_map/reduce_scatter | solution.py:248
  526.3 104.9 %copy-start.55 = (u32[32]{0:T(128)S(1)}, u32[32]{0:T(128)}, u32[]{:S(2)}) copy-start(u32[32]{0:T(128)} %constant.178) | copy-start | bytes 388
  526.3 106.7 %copy-start.43 = (f32[4,128]{1,0:T(4,128)S(1)}, f32[4,128]{1,0:T(4,128)}, u32[]{:S(2)}) copy-start(f32[4,128]{1,0:T(4,128)} %copy-done.42) | copy-start | bytes 6148
  526.3 106.8 %copy-start.17 = (bf16[4,128,640]{2,1,0:T(8,128)(2,1)S(1)}, bf16[4,128,640]{2,1,0:T(8,128)(2,1)}, u32[]{:S(2)}) copy-start(bf16[4,128,640]{2,1,0:T(8,128)(2,1)} %param.10) | copy-start | bytes 1966084
  526.3 106.8 %copy-start.25 = (bf16[4,128,6,256]{1,0,3,2:T(4,128)(2,1)S(1)}, bf16[4,128,6,256]{1,0,3,2:T(4,128)(2,1)}, u32[]{:S(2)}) copy-start(bf16[4,128,6,256]{1,0,3,2:T(4,128)(2,1)} %copy-done.24) | copy-start | bytes 4718596
  526.4 106.8 %copy-start.38 = (f32[640]{0:T(1024)S(1)}, f32[640]{0:T(1024)}, u32[]{:S(2)}) copy-start(f32[640]{0:T(1024)} %copy-done.37) | copy-start | bytes 7684
  526.4 201.2 %reduce-scatter.29.cloned.1.call-start = ((), (), s32[]{:S(2)}) async-start(), calls=%async_computation.22 | async-start | bytes 737280
  568.9 192.2 %reduce-scatter.21.cloned.1.call-start = ((), (), s32[]{:S(2)}) async-start(), calls=%async_computation.17 | async-start | bytes 1474560 | tf_op jit(solution)/shard_map/reduce_scatter | solution.py:254
  633.2 38.2 %copy-start.14 = (f32[512,640]{1,0:T(8,128)S(1)}, f32[512,640]{1,0:T(8,128)}, u32[]{:S(2)}) copy-start(f32[512,640]{1,0:T(8,128)} %copy-done.13) | copy-start | bytes 3932164
  (55 other events, 218.5 us)
Sparse Core Ops, SparseCore 0:
  25.2 35.3 all-gather.9
  62.2 25.5 all-gather.15
  90.0 30.7 all-gather.11
  122.8 28.0 all-gather.21
  152.6 28.1 all-gather.13
  182.5 61.4 all-gather.17
  245.8 39.4 all-gather.19
  326.5 29.3 reduce-scatter.16
  491.3 32.8 reduce-scatter.24
  527.1 39.5 reduce-scatter.22
  569.7 61.4 reduce-scatter.18
  633.8 30.5 reduce-scatter.26
  666.8 29.1 reduce-scatter.14
  698.1 29.4 reduce-scatter.28
  729.7 31.3 reduce-scatter.20
where the time goes:
time: 772 us; the launch traced here: 770 us
  waiting for transfers between devices  373 us (48%)
  matrix products  129 us (17%)
  blocking collectives  101 us (13%)
  local copies, waits for them, and re-layouts  69.2 us (9%)
  other arithmetic  64 us (8%)
  between operations  17 us (2%)
  starting transfers between devices  15.6 us (2%)
    reduce_scatter x1, waiting for transfers between devices, body(): lax.psum_scatter(grad_gu.astype(jnp.bfloat16), 'batch', scatter_dimension...  62.2 us
    all_gather x1, waiting for transfers between devices, body(): lax.all_gather(part_gu, 'batch', axis=1, tiled=True)  58.5 us
    unnamed x18, waiting for transfers between devices  48.3 us
    unnamed x3, blocking collectives  40.5 us
    reduce_scatter x1, waiting for transfers between devices, body(): lax.psum_scatter(grad_down.astype(jnp.bfloat16), 'batch', scatter_dimensi...  40.1 us
    unnamed x132, local copies, waits for them, and re-layouts  39.4 us
    reduce_scatter x1, waiting for transfers between devices, body(): lax.psum_scatter(sum_gu.astype(jnp.bfloat16), 'ctx', scatter_dimension=0,...  31.7 us
    all_gather x1, waiting for transfers between devices, body(): lax.all_gather(part_down, 'batch', axis=0, tiled=True)  30.1 us
  transfers between devices with their start and end apart: 47, of which 29 were waited for; matrix products, arithmetic and copies ran while one was open for 26% of the time, Pallas kernels for 0%

commit v1 on v0

--- a/solution.py
+++ b/solution.py
@@ -1,6 +1,8 @@
 import jax
 import jax.numpy as jnp
 from jax import lax
+from jax.experimental import pallas as pl
+from jax.experimental.pallas import tpu as pltpu
 from jax.sharding import PartitionSpec as P
 
 D = 640
@@ -12,12 +14,6 @@
 rope_base = 1000000.0
 epsilon = 1e-06
 neg_large = -1e30
-
-
-def passed_along(value, axis, steps):
-    count = lax.axis_size(axis)
-    pairs = [(source, (source + steps) % count) for source in range(count)]
-    return lax.ppermute(value, axis, pairs)
 
 
 def rms_scale(values, gain_vec):
@@ -62,26 +58,158 @@
     return gelu_tanh(gate_up[:, :FF]) * gate_up[:, FF:]
 
 
+MESH = pl.DeviceIdType.MESH
+
+
+def flip(index, bit):
+    half = (index // bit) % 2
+    return index + bit - 2 * bit * half
+
+
+def greet(others):
+    barrier = pltpu.get_barrier_semaphore()
+    for other in others:
+        pl.semaphore_signal(barrier, inc=1, device_id=other, device_id_type=MESH)
+    pl.semaphore_wait(barrier, len(others))
+
+
+def gather_kernel(chips, *refs):
+    count = (len(refs) - 3) // 2
+    shards, wholes = refs[:count], refs[count : 2 * count]
+    own_sem, send_sem, recv_sem = refs[2 * count :]
+    mine = lax.axis_index("batch")
+    place = lax.axis_index("ctx")
+    lane, chip = place % 2, place // 2
+    mate = flip(place, 1)
+    over_x, over_y = flip(mine, 1), flip(mine, 2)
+    corner = flip(over_x, 2)
+    line = [place] + [((chip + d) % chips) * 2 + lane for d in range(1, chips)]
+    greet(
+        [(mine, mate), (over_x, place), (over_y, place)] + [(mine, there) for there in line[1:]]
+    )
+
+    def window(which, row_owner, place_owner):
+        whole = wholes[which]
+        rows, width = shards[which].shape
+        if which == 0:
+            start = pl.multiple_of((row_owner * (2 * chips) + place_owner) * rows, rows)
+            return whole.at[pl.ds(start, rows), :]
+        return whole.at[
+            pl.ds(pl.multiple_of(place_owner * rows, rows), rows),
+            pl.ds(pl.multiple_of(row_owner * width, 128), width),
+        ]
+
+    sent = []
+    used = [0] * count
+
+    def send(which, row_owner, place_owner, target, source=None):
+        copy = pltpu.make_async_remote_copy(
+            src_ref=window(which, row_owner, place_owner) if source is None else source,
+            dst_ref=window(which, row_owner, place_owner),
+            send_sem=send_sem.at[which, used[which]],
+            recv_sem=recv_sem.at[which, row_owner, place_owner],
+            device_id=target,
+            device_id_type=MESH,
+        )
+        used[which] += 1
+        copy.start()
+        sent.append(copy)
+
+    def arrived(which, row_owner, place_owner):
+        pltpu.make_async_copy(
+            window(which, row_owner, place_owner),
+            window(which, row_owner, place_owner),
+            recv_sem.at[which, row_owner, place_owner],
+        ).wait()
+
+    first = [over_x] * (count - 1) + [over_y]
+    second = [over_y] * (count - 1) + [over_x]
+    own = []
+    for which in range(count):
+        copy = pltpu.make_async_copy(
+            shards[which], window(which, mine, place), own_sem.at[which]
+        )
+        copy.start()
+        own.append(copy)
+        source = shards[which]
+        for there in line[1:]:
+            send(which, mine, place, (mine, there), source)
+        send(which, mine, place, (first[which], place), source)
+        send(which, mine, place, (second[which], place), source)
+        send(which, mine, place, (mine, mate), source)
+    for step in range(chips):
+        for which in range(count):
+            if step > 0:
+                arrived(which, mine, line[step])
+                send(which, mine, line[step], (first[which], place))
+                send(which, mine, line[step], (second[which], place))
+                send(which, mine, line[step], (mine, mate))
+        for which in range(count):
+            arrived(which, first[which], line[step])
+            send(which, first[which], line[step], (second[which], place))
+            send(which, first[which], line[step], (mine, mate))
+    for step in range(chips):
+        for which in range(count):
+            arrived(which, second[which], line[step])
+            send(which, second[which], line[step], (mine, mate))
+        for which in range(count):
+            arrived(which, corner, line[step])
+            send(which, corner, line[step], (mine, mate))
+    for step in range(chips):
+        for which in range(count):
+            for row_owner in (mine, over_x, over_y, corner):
+                arrived(which, row_owner, flip(line[step], 1))
+    for copy in own:
+        copy.wait()
+    for copy in sent:
+        copy.wait_send()
+
+
+def gather_weights(w_qkv, w_out, w_gate_up, w_down, norm_gains):
+    groups, places = lax.axis_size("batch"), lax.axis_size("ctx")
+    chips = places // 2
+    rows = w_qkv.shape[0]
+    if groups != 4 or rows % 16 != 0 or chips < 2:
+        full = (
+            lax.all_gather(lax.all_gather(w_qkv, "ctx", axis=0, tiled=True), "batch", axis=1, tiled=True),
+            lax.all_gather(lax.all_gather(w_out, "ctx", axis=1, tiled=True), "batch", axis=0, tiled=True).T,
+            lax.all_gather(lax.all_gather(w_gate_up, "ctx", axis=0, tiled=True), "batch", axis=1, tiled=True),
+            lax.all_gather(lax.all_gather(w_down, "ctx", axis=1, tiled=True), "batch", axis=0, tiled=True).T,
+            lax.all_gather(norm_gains, ("batch", "ctx"), axis=0, tiled=True),
+        )
+        return full
+    gain_count = norm_gains.shape[0]
+    gain_tile = jnp.pad(norm_gains[None, :], ((0, 15), (0, 128 - gain_count)))
+    shards = (gain_tile, w_qkv, w_out.T, w_down.T, w_gate_up)
+    shapes = [(groups * places * 16, 128)] + [
+        (places * piece.shape[0], groups * piece.shape[1]) for piece in shards[1:]
+    ]
+    any_space = pl.BlockSpec(memory_space=pl.ANY)
+    sends = 2 + chips + 2 * (chips - 1) + (4 * chips) + 2 * chips + 4
+    gains, qkv, out_t, down_t, gate_up = pl.pallas_call(
+        lambda *refs: gather_kernel(chips, *refs),
+        out_shape=[jax.ShapeDtypeStruct(shape, jnp.bfloat16) for shape in shapes],
+        in_specs=[any_space] * 5,
+        out_specs=[any_space] * 5,
+        scratch_shapes=[
+            pltpu.SemaphoreType.DMA((5,)),
+            pltpu.SemaphoreType.DMA((5, sends)),
+            pltpu.SemaphoreType.DMA((5, groups, places)),
+        ],
+        compiler_params=pltpu.CompilerParams(collective_id=0, has_side_effects=True),
+        name="gather_weights",
+    )(*shards)
+    gains = gains.reshape(groups * places, 16, 128)[:, 0, :gain_count].reshape(-1)
+    return qkv, out_t, gate_up, down_t, gains
+
+
 def body(tokens, w_qkv, w_out, w_gate_up, w_down, norm_gains, block_order, cotangent):
     seq_count, tok_rows, _ = tokens.shape
     block_len = tok_rows // 2
-    ctx_size = lax.axis_size("ctx")
     ctx_index = lax.axis_index("ctx")
     score_scale = HD ** (-0.5)
-    ctx_parts = (
-        lax.all_gather(w_qkv, "ctx", axis=0, tiled=True),
-        lax.all_gather(w_out, "ctx", axis=1, tiled=True),
-        lax.all_gather(w_gate_up, "ctx", axis=0, tiled=True),
-        lax.all_gather(w_down, "ctx", axis=1, tiled=True),
-        lax.all_gather(norm_gains, "ctx", axis=0, tiled=True),
-    )
-    part_qkv, part_out, part_gu, part_down, part_gains = ctx_parts
-    full_qkv, full_out, full_gu, full_down, full_gains = (
-        lax.all_gather(part_qkv, "batch", axis=1, tiled=True),
-        lax.all_gather(part_out, "batch", axis=0, tiled=True),
-        lax.all_gather(part_gu, "batch", axis=1, tiled=True),
-        lax.all_gather(part_down, "batch", axis=0, tiled=True),
-        lax.all_gather(part_gains, "batch", axis=0, tiled=True),
+    full_qkv, full_out, full_gu, full_down, full_gains = gather_weights(
+        w_qkv, w_out, w_gate_up, w_down, norm_gains
     )
     gain_all = full_gains.astype(jnp.float32)
     gain_in = gain_all[0:D]
@@ -114,50 +242,40 @@
     key_b = key_vecs.astype(jnp.bfloat16)
     value_b = val_vecs.astype(jnp.bfloat16)
 
-    def scores_for(key_piece, piece_pos):
-        allowed = piece_pos[None, :] <= query_pos[:, None]
-        raw_scores = (
-            jnp.einsum("shrd,snd->shrn", query_b, key_piece, preferred_element_type=jnp.float32)
-            * score_scale
-        )
-        return (jnp.where(allowed, raw_scores, neg_large), allowed)
-
-    stat_shape = (seq_count, H, tok_rows)
-    row_max = jnp.full(stat_shape, neg_large, jnp.float32)
-    key_piece = lax.all_gather(key_b, "ctx", axis=1, tiled=True)
-    value_piece = lax.all_gather(value_b, "ctx", axis=1, tiled=True)
-    piece_pos = key_pos
-    scores, allowed = scores_for(key_piece, piece_pos)
-    new_max = jnp.maximum(row_max, jnp.max(scores, axis=-1))
-    powers = jnp.where(allowed, jnp.exp(scores - new_max[..., None]), 0.0)
-    row_total = jnp.sum(powers, axis=-1)
-    weighted = jnp.einsum(
-        "shrn,snd->shrd",
-        powers.astype(jnp.bfloat16),
-        value_piece,
-        preferred_element_type=jnp.float32,
-    )
-    row_max, row_total, weighted = (new_max, row_total, weighted)
-    attn_out = weighted / row_total[..., None]
-    log_total = row_max + jnp.log(row_total)
+    key_value = lax.all_gather(
+        jnp.concatenate([key_b, value_b], axis=-1), "ctx", axis=1, tiled=True
+    )
+    key_piece, value_piece = key_value[..., :HD], key_value[..., HD:]
+    allowed = key_pos[None, :] <= query_pos[:, None]
+    raw_scores = (
+        jnp.einsum("shrd,snd->shrn", query_b, key_piece, preferred_element_type=jnp.float32)
+        * score_scale
+    )
+    scores = jnp.where(allowed, raw_scores, neg_large)
+    row_max = jnp.max(scores, axis=-1, keepdims=True)
+    powers = jnp.exp(scores - row_max)
+    soft_b = (powers / jnp.sum(powers, axis=-1, keepdims=True)).astype(jnp.bfloat16)
+    attn_out = jnp.einsum(
+        "shrn,snd->shrd", soft_b, value_piece, preferred_element_type=jnp.float32
+    )
     attn_b = (
         attn_out.transpose(0, 2, 1, 3).reshape(seq_count * tok_rows, H * HD).astype(jnp.bfloat16)
     )
-    y_attn = jnp.dot(attn_b, full_out, preferred_element_type=jnp.float32)
+    y_attn = jnp.einsum("te,de->td", attn_b, full_out, preferred_element_type=jnp.float32)
     residual, back_attn = jax.vjp(add_branch, y_attn, flat, gain_attn)
     normed_two, back_two = jax.vjp(rms_scale, residual, gain_pre)
     normed_two_b = normed_two.astype(jnp.bfloat16)
     gate_up = jnp.dot(normed_two_b, full_gu, preferred_element_type=jnp.float32)
     hidden, back_act = jax.vjp(activate, gate_up)
     hidden_b = hidden.astype(jnp.bfloat16)
-    branch = jnp.dot(hidden_b, full_down, preferred_element_type=jnp.float32)
+    branch = jnp.einsum("tf,df->td", hidden_b, full_down, preferred_element_type=jnp.float32)
     output, back_out = jax.vjp(add_branch, branch, residual, gain_post)
     result = output.astype(jnp.bfloat16).reshape(tokens.shape)
     seed_grad = cotangent.reshape(seq_count * tok_rows, D).astype(jnp.float32)
     d_branch, d_resid_a, d_gain_post = back_out(seed_grad)
     d_branch_b = d_branch.astype(jnp.bfloat16)
     grad_down = jnp.einsum("tf,td->fd", hidden_b, d_branch_b, preferred_element_type=jnp.float32)
-    d_hidden = jnp.einsum("td,fd->tf", d_branch_b, full_down, preferred_element_type=jnp.float32)
+    d_hidden = jnp.einsum("td,df->tf", d_branch_b, full_down, preferred_element_type=jnp.float32)
     (d_gate_up,) = back_act(d_hidden)
     d_gate_up_b = d_gate_up.astype(jnp.bfloat16)
     grad_gu = jnp.einsum("td,tf->df", normed_two_b, d_gate_up_b, preferred_element_type=jnp.float32)
@@ -167,56 +285,31 @@
     d_y_attn_b = d_y_attn.astype(jnp.bfloat16)
     grad_out = jnp.einsum("te,td->ed", attn_b, d_y_attn_b, preferred_element_type=jnp.float32)
     d_attn_rows = jnp.einsum(
-        "td,ed->te", d_y_attn_b, full_out, preferred_element_type=jnp.float32
+        "td,de->te", d_y_attn_b, full_out, preferred_element_type=jnp.float32
     ).astype(jnp.bfloat16)
     d_attn = d_attn_rows.reshape(seq_count, tok_rows, H, HD).transpose(0, 2, 1, 3)
     row_dot = jnp.sum(d_attn.astype(jnp.float32) * attn_out, axis=-1)
 
-    def piece_grads(key_piece, value_piece, piece_pos):
-        scores, allowed = scores_for(key_piece, piece_pos)
-        soft_probs = jnp.where(allowed, jnp.exp(scores - log_total[..., None]), 0.0)
-        d_probs = jnp.einsum(
-            "shrd,snd->shrn", d_attn, value_piece, preferred_element_type=jnp.float32
-        )
-        d_scores = (soft_probs * (d_probs - row_dot[..., None])).astype(jnp.bfloat16)
-        d_query = (
-            jnp.einsum("shrn,snd->shrd", d_scores, key_piece, preferred_element_type=jnp.float32)
-            * score_scale
-        )
-        d_key = (
-            jnp.einsum("shrn,shrd->snd", d_scores, query_b, preferred_element_type=jnp.float32)
-            * score_scale
-        )
-        d_value = jnp.einsum(
-            "shrn,shrd->snd",
-            soft_probs.astype(jnp.bfloat16),
-            d_attn,
-            preferred_element_type=jnp.float32,
-        )
-        return (d_query, d_key, d_value)
-
-    def cycle_turn(turn_index, loop_state):
-        key_piece, value_piece, sum_key, sum_value, sum_query = loop_state
-        owner_index = (ctx_index - turn_index) % ctx_size
-        piece_pos = lax.dynamic_slice_in_dim(key_pos, owner_index * tok_rows, tok_rows)
-        d_query, d_key, d_value = piece_grads(key_piece, value_piece, piece_pos)
-        key_piece, value_piece = passed_along((key_piece, value_piece), "ctx", 1)
-        sum_key, sum_value = (
-            passed_along((sum_key + d_key).astype(jnp.bfloat16), "ctx", 1).astype(jnp.float32),
-            passed_along((sum_value + d_value).astype(jnp.bfloat16), "ctx", 1).astype(jnp.float32),
-        )
-        return (key_piece, value_piece, sum_key, sum_value, sum_query + d_query)
-
-    zero_kv = jnp.zeros(key_b.shape, jnp.float32)
-    final_state = lax.fori_loop(
-        0,
-        ctx_size,
-        cycle_turn,
-        (key_b, value_b, zero_kv, zero_kv, jnp.zeros(query_b.shape, jnp.float32)),
-    )
-    grad_key = final_state[2]
-    grad_value = final_state[3]
-    grad_query = final_state[4]
+    d_probs = jnp.einsum(
+        "shrd,snd->shrn", d_attn, value_piece, preferred_element_type=jnp.float32
+    )
+    d_scores = (soft_b.astype(jnp.float32) * (d_probs - row_dot[..., None])).astype(jnp.bfloat16)
+    d_key = (
+        jnp.einsum("shrn,shrd->snd", d_scores, query_b, preferred_element_type=jnp.float32)
+        * score_scale
+    )
+    d_value = jnp.einsum("shrn,shrd->snd", soft_b, d_attn, preferred_element_type=jnp.float32)
+    d_key_value = lax.psum_scatter(
+        jnp.concatenate([d_key, d_value], axis=-1).astype(jnp.bfloat16),
+        "ctx",
+        scatter_dimension=1,
+        tiled=True,
+    ).astype(jnp.float32)
+    grad_key, grad_value = d_key_value[..., :HD], d_key_value[..., HD:]
+    grad_query = (
+        jnp.einsum("shrn,snd->shrd", d_scores, key_piece, preferred_element_type=jnp.float32)
+        * score_scale
+    )
     d_projected, d_gain_query, d_gain_key = back_prep((grad_query, grad_key, grad_value))
     d_projected_b = d_projected.astype(jnp.bfloat16)
     grad_qkv = jnp.einsum("td,te->de", normed_b, d_projected_b, preferred_element_type=jnp.float32)

time: 772 us -> 556 us (0.72)
  blocking collectives: 101 us -> 23.5 us
  waiting for transfers between devices: 373 us -> 306 us
  matrix products: 129 us -> 63.3 us
  Pallas kernels: 0 us -> 63.7 us
  local copies, waits for them, and re-layouts: 69.2 us -> 32.8 us
  other arithmetic: 64 us -> 41.4 us
  starting transfers between devices: 15.6 us -> 0.41 us
    all_gather x7 -> x1, waiting for transfers between devices: 146 us -> 53.1 us  [body(): lax.all_gather(jnp.concatenate([key_b, value_b], axis=-1), 'ctx', axis=1,...]
    dot_general x46 -> x10, matrix products: 93.4 us -> 28.2 us  [the longest x1 5.74 us: body(): jnp.einsum('td,df->tf', d_branch_b, full_down, preferred_element_type=jnp...]
    pallas_call x0 -> x1, Pallas kernels: none -> 63.7 us  [gather_weights(): pl.pallas_call(lambda *refs: gather_kernel(chips, *refs), out_shape=[jax....]
    all_gather x4 -> x0, blocking collectives: 60.2 us -> none  [the longest x1 17.8 us: body(): lax.all_gather(w_qkv, 'ctx', axis=0, tiled=True)]
    reduce_scatter x0 -> x1, waiting for transfers between devices: none -> 49.9 us  [body(): lax.psum_scatter(jnp.concatenate([d_key, d_value], axis=-1).astype(jnp.bf...]
    unnamed x18 -> x13, waiting for transfers between devices: 48.3 us -> 94.8 us
    reduce_scatter x1, waiting for transfers between devices: 31.7 us -> 0.91 us  [body(): lax.psum_scatter(sum_gu.astype(jnp.bfloat16), 'ctx', scatter_dimension=0,...]
    convert_element_type x17 -> x3, other arithmetic: 28.6 us -> 2.89 us  [the longest x1 1.61 us: body(): (powers / jnp.sum(powers, axis=-1, keepdims=True)).astype(jnp.bfloat16)]
  transfers between devices with their start and end apart: 47 -> 10, of which waited for: 29 -> 9; matrix products, arithmetic and copies ran while one was open for 26% -> 14% of each run, Pallas kernels for 0% -> 0%
where the time goes in v1:
time: 556 us; the launch traced here: 547 us
  waiting for transfers between devices  306 us (55%)
  Pallas kernels  63.7 us (11%)
  matrix products  63.3 us (11%)
  other arithmetic  41.4 us (7%)
  local copies, waits for them, and re-layouts  32.8 us (6%)
  blocking collectives  23.5 us (4%)
  between operations  16.6 us (3%)
    unnamed x13, waiting for transfers between devices  94.8 us
    pallas_call x1, Pallas kernels, gather_weights(): pl.pallas_call(lambda *refs: gather_kernel(chips, *refs), out_shape=[jax....  63.7 us
    all_gather x1, waiting for transfers between devices, body(): lax.all_gather(jnp.concatenate([key_b, value_b], axis=-1), 'ctx', axis=1,...  53.1 us
    reduce_scatter x1, waiting for transfers between devices, body(): lax.psum_scatter(grad_gu.astype(jnp.bfloat16), 'batch', scatter_dimension...  51.9 us
    reduce_scatter x1, waiting for transfers between devices, body(): lax.psum_scatter(jnp.concatenate([d_key, d_value], axis=-1).astype(jnp.bf...  49.9 us
    reduce_scatter x1, waiting for transfers between devices, body(): lax.psum_scatter(sum_qkv.astype(jnp.bfloat16), 'ctx', scatter_dimension=0...  29.6 us
    reduce_scatter x1, waiting for transfers between devices, body(): lax.psum_scatter(grad_down.astype(jnp.bfloat16), 'batch', scatter_dimensi...  25.4 us
    unnamed x2, blocking collectives  23.5 us
  transfers between devices with their start and end apart: 10, of which 9 were waited for; matrix products, arithmetic and copies ran while one was open for 14% of the time, Pallas kernels for 0%

profile of v1, /device:TPU:0, one launch (start us, length us, event | category | flops | bytes accessed | tf_op | source)
XLA Modules:
  0.0 547.5 jit_solution(3518246487746626539)
XLA Ops:
  7.2 1.3 pad.31.refs_0_
  8.5 63.7 %gather_weights.1 = (bf16[512,128]{1,0:T(8,128)(2,1)}, bf16[640,1536]{1,0:T(8,128)(2,1)}, bf16[640,1024]{1,0:T(8,128)(2,1)}, bf16[640,2048]{1,0:T(8,128)(2,1)}, bf16[640,4096]{1,0:T(8,128)(2,1)}) custom-call(bf16[16,128]{1,0:T(8,128)(2,1)} %pad.31.refs_0_, bf16[80,384]{1,0:T(8,128)(2,1)} %refs_1_.1, bf16[80,256]{1,0:T(8,128)(2,1)} %bitcast.164, ...), custom_call_target="tpu_custom_call" | custom-call | tf_op jit(solution)/shard_map/gather_weights/pallas_call | solution.py:189
  72.2 1.0 fusion.53
  73.8 4.0 copy.40
  78.5 3.2 fusion.48
  82.7 0.9 multiply_multiply_fusion.3
  84.2 1.0 multiply_cosine_fusion
  85.2 1.1 subtract_convert_fusion.1
  86.3 0.8 pad_maximum_fusion.1
  88.4 1.0 multiply_multiply_fusion.2
  89.4 1.3 subtract_convert_fusion
  90.7 53.1 %all-gather.2.cloned.1.call-done = bf16[4,1024,512]{2,1,0:T(8,128)(2,1)} async-done(((bf16[4,128,512]{2,1,0:T(8,128)(2,1)}), bf16[4,1024,512]{2,1,0:T(8,128)(2,1)}) %all-gather.2.cloned.1.call-update) | async-done | bytes 4194320 | tf_op jit(solution)/shard_map/all_gather | solution.py:245
  143.8 3.2 fusion.13
  147.0 3.7 fusion.66
  150.8 1.6 divide_convert_fusion
  153.0 1.3 fusion.18
  156.7 1.4 copy-done.38
  158.2 1.1 multiply_reduce_fusion.10
  159.8 3.5 fusion.64
  163.3 1.5 multiply_convert_fusion.1
  165.0 1.9 multiply_reduce_fusion.8
  167.5 1.4 fusion.32
  168.9 5.7 %fusion.28 = (f32[512,2048]{1,0:T(8,128)S(1)}, f32[512,2048]{1,0:T(8,128)S(1)}) fusion(f32[512,4096]{1,0:T(8,128)S(1)} %fusion.64, bf16[512,640]{1,0:T(8,128)(2,1)S(1)} %get-tuple-element.61, bf16[640,2048]{1,0:T(8,128)(2,1)S(1)} %copy-done.37), kind=kOutput, calls=%fused_computation.60 | convolution fusion | flops 1369440256 | bytes 20054016 | tf_op jit(solution)/shard_map/td,df->tf/dot_general | solution.py:278
  174.7 4.6 multiply_reduce_fusion.4
  179.3 2.2 multiply_reduce_fusion.5
  182.5 0.9 copy-done.26
  183.4 2.1 convolution_convert_fusion.3
  185.6 5.1 convolution_convert_fusion.1
  190.8 3.5 convolution_convert_fusion.4
  194.2 2.8 reshape.322
  197.1 2.4 multiply_reduce_fusion.2
  199.5 4.1 bitcast_convert_fusion
  203.6 1.6 multiply_convert_fusion
  205.3 1.7 fusion.7
  207.2 2.4 pad_maximum_fusion
  209.7 9.2 %convolution_convert_fusion = bf16[640,4096]{1,0:T(8,128)(2,1)} fusion(f32[512,2048]{1,0:T(8,128)} %copy-done.12, f32[512,2048]{1,0:T(8,128)} %copy-done.11, f32[512,640]{1,0:T(8,128)} %copy-done, f32[640]{0:T(1024)S(1)} %get-tuple-element.68, f32[512]{0:T(512)S(1)} %fusion.57), kind=kOutput, calls=%fused_computation.7 | convolution fusion | flops 2692153344 | bytes 14946816 | tf_op jit(solution)/shard_map/td,tf->df/dot_general | solution.py:281
  219.0 4.1 multiply_bitcast_fusion
  223.1 1.6 multiply_add_fusion.3
  224.7 1.9 copy.70
  226.7 2.4 multiply_reduce_fusion
  229.2 1.7 add_add_fusion
  230.9 25.4 %reduce-scatter.26.cloned.1.call-done = bf16[512,640]{1,0:T(8,128)(2,1)} async-done(((bf16[2048,640]{1,0:T(8,128)(2,1)}), bf16[512,640]{1,0:T(8,128)(2,1)}) %reduce-scatter.26.cloned.1.call-update) | async-done | bytes 655376 | tf_op jit(solution)/shard_map/reduce_scatter | solution.py:332
  256.3 2.2 copy.72
  258.5 49.9 %reduce-scatter.16.cloned.1.call-done = bf16[4,128,512]{2,1,0:T(8,128)(2,1)} async-done(((bf16[4,1024,512]{2,1,0:T(8,128)(2,1)}), bf16[4,128,512]{2,1,0:T(8,128)(2,1)}) %reduce-scatter.16.cloned.1.call-update) | async-done | bytes 524304 | tf_op jit(solution)/shard_map/reduce_scatter | solution.py:302
  308.5 1.2 convert_element_type.160
  310.3 1.1 copy-done.9
  311.5 2.5 copy.51
  314.0 2.6 convolution_convert_fusion.2
  316.7 2.3 copy.68
  319.1 51.9 %reduce-scatter.22.cloned.1.call-done = bf16[640,1024]{1,0:T(8,128)(2,1)} async-done(((bf16[640,4096]{1,0:T(8,128)(2,1)}), bf16[640,1024]{1,0:T(8,128)(2,1)}) %reduce-scatter.22.cloned.1.call-update) | async-done | bytes 1310736 | tf_op jit(solution)/shard_map/reduce_scatter | solution.py:329
  373.5 30.6 %reduce-scatter.30.cloned.1.call-done = bf16[80,256]{1,0:T(8,128)(2,1)} async-done(((bf16[640,256]{1,0:T(8,128)(2,1)}), bf16[80,256]{1,0:T(8,128)(2,1)}) %reduce-scatter.30.cloned.1.call-update) | async-done | bytes 40976
  404.2 0.9 copy.71
  405.8 30.2 %reduce-scatter.32.cloned.1.call-done = bf16[80,512]{1,0:T(8,128)(2,1)} async-done(((bf16[640,512]{1,0:T(8,128)(2,1)}), bf16[80,512]{1,0:T(8,128)(2,1)}) %reduce-scatter.32.cloned.1.call-update) | async-done | bytes 81936
  436.0 1.0 copy.73
  437.8 33.9 %reduce-scatter.28.cloned.1.call-done = bf16[384,640]{1,0:T(8,128)(2,1)} async-done(((bf16[1536,640]{1,0:T(8,128)(2,1)}), bf16[384,640]{1,0:T(8,128)(2,1)}) %reduce-scatter.28.cloned.1.call-update) | async-done | bytes 491536
  471.6 2.0 copy.69
  473.7 4.8 fusion.41
  479.6 9.0 %all-reduce.10 = bf16[3072]{0:T(1024)(128)(2,1)S(1)} all-reduce(bf16[3072]{0:T(1024)(128)(2,1)S(1)} %dynamic-update-slice.5), channel_id=11, replica_groups=mesh['batch'=4,'ctx'=8] {'batch'}, use_global_device_ids=true, to_apply=%region_30.31.clone | all-reduce | flops 3072 | bytes 12288
  488.8 14.4 %all-reduce.11 = bf16[768]{0:T(1024)(128)(2,1)S(1)} all-reduce(bf16[768]{0:T(1024)(128)(2,1)S(1)} %dynamic-slice.1), channel_id=12, replica_groups=mesh['batch'=4,'ctx'=8] {'ctx'}, use_global_device_ids=true, to_apply=%region_31.32.clone | all-reduce | flops 768 | bytes 3072
  503.8 2.7 fusion.34
  506.5 0.9 reduce-scatter.24.cloned.1.call-done
  507.4 1.7 convert_element_type.169
  509.1 29.6 %reduce-scatter.18.cloned.1.call-done = bf16[80,384]{1,0:T(8,128)(2,1)} async-done(((bf16[640,384]{1,0:T(8,128)(2,1)}), bf16[80,384]{1,0:T(8,128)(2,1)}) %reduce-scatter.18.cloned.1.call-update) | async-done | bytes 61456 | tf_op jit(solution)/shard_map/reduce_scatter | solution.py:341
  538.7 1.5 convert_element_type.165
  (159 shorter events, 15.7 us)
Async XLA Ops:
  7.2 136.6 %all-gather.2.cloned.1.call-start = ((), (), s32[]{:S(2)}) async-start(), calls=%async_computation.9 | async-start | bytes 4718592 | tf_op jit(solution)/shard_map/all_gather | solution.py:245
  72.2 5.6 %copy-start.3 = (bf16[4,128,640]{2,1,0:T(8,128)(2,1)S(1)}, bf16[4,128,640]{2,1,0:T(8,128)(2,1)}, u32[]{:S(2)}) copy-start(bf16[4,128,640]{2,1,0:T(8,128)(2,1)} %param.8) | copy-start | bytes 1966084
  73.8 8.9 %copy-start.34 = (f32[256]{0:T(256)}, f32[256]{0:T(256)S(1)}, u32[]{:S(2)}) copy-start(f32[256]{0:T(256)S(1)} %get-tuple-element.72) | copy-start | bytes 3076
  78.0 0.6 copy-start.29
  78.5 3.2 copy-start.24
  78.5 4.0 copy-start.39
  82.0 0.6 copy-start.32
  82.5 1.7 copy-start.27
  82.7 1.5 copy-start.31
  87.2 137.6 %reduce-scatter.20.cloned.1.call-start = ((), (), s32[]{:S(2)}) async-start(), calls=%async_computation.12 | async-start | bytes 1638400 | tf_op jit(solution)/shard_map/reduce_scatter | solution.py:326
  150.8 2.2 copy-start.21
  152.9 2.1 copy-start.14
  153.0 6.8 %slice-start = ((s8[5242880]{0:T(1024)(128)(4,1)}), s8[4194304]{0:T(1024)(128)(4,1)S(1)}, s32[]{:S(2)}) async-start(s8[5242880]{0:T(1024)(128)(4,1)} %bitcast.146), calls=%async_computation.19 | async-start | bytes 8388608
  155.1 1.4 copy-start.8
  155.2 2.9 copy-start.38
  155.2 4.5 slice-start.1
  156.7 2.6 copy-start.19
  158.2 1.1 copy-start.4
  159.7 19.6 %copy-start = (f32[512,640]{1,0:T(8,128)}, f32[512,640]{1,0:T(8,128)S(1)}, u32[]{:S(2)}) copy-start(f32[512,640]{1,0:T(8,128)S(1)} %get-tuple-element.52) | copy-start | bytes 3932164
  163.3 1.7 copy-start.37
  164.8 2.2 copy-start.16
  165.0 1.9 copy-start.10
  168.9 5.8 %copy-start.23 = (bf16[512,640]{1,0:T(8,128)(2,1)}, bf16[512,640]{1,0:T(8,128)(2,1)S(1)}, u32[]{:S(2)}) copy-start(bf16[512,640]{1,0:T(8,128)(2,1)S(1)} %get-tuple-element.61) | copy-start | bytes 1966084
  174.7 4.6 copy-start.11
  174.7 4.6 copy-start.12
  181.5 1.1 copy-start.1
  181.5 1.9 copy-start.20
  182.5 0.9 copy-start.26
  185.5 70.8 %reduce-scatter.26.cloned.1.call-start = ((), (), s32[]{:S(2)}) async-start(), calls=%async_computation.15 | async-start | bytes 3276800 | tf_op jit(solution)/shard_map/reduce_scatter | solution.py:332
  190.7 117.8 %reduce-scatter.16.cloned.1.call-start = ((), (), s32[]{:S(2)}) async-start(), calls=%async_computation.10 | async-start | bytes 4718592 | tf_op jit(solution)/shard_map/reduce_scatter | solution.py:302
  197.1 2.4 copy-start.13
  197.1 6.5 %copy-start.22 = (bf16[4,1024,512]{2,1,0:T(8,128)(2,1)S(1)}, bf16[4,1024,512]{2,1,0:T(8,128)(2,1)}, u32[]{:S(2)}) copy-start(bf16[4,1024,512]{2,1,0:T(8,128)(2,1)} %all-gather.2.cloned.1.call-done) | copy-start | bytes 12582916
  199.5 4.1 copy-start.15
  203.6 1.7 copy-start.17
  203.6 1.7 copy-start.18
  205.3 2.0 copy-start.42
  209.7 161.3 %reduce-scatter.22.cloned.1.call-start = ((), (), s32[]{:S(2)}) async-start(), calls=%async_computation.13 | async-start | bytes 6553600 | tf_op jit(solution)/shard_map/reduce_scatter | solution.py:329
  218.9 185.2 %reduce-scatter.30.cloned.1.call-start = ((), (), s32[]{:S(2)}) async-start(), calls=%async_computation.17 | async-start | bytes 368640
  223.1 3.6 copy-start.36
  226.6 209.3 %reduce-scatter.32.cloned.1.call-start = ((), (), s32[]{:S(2)}) async-start(), calls=%async_computation.18 | async-start | bytes 737280
  226.7 2.5 copy-start.6
  226.7 2.5 copy-start.7
  230.9 78.9 %copy-start.28 = (f32[4,128]{1,0:T(4,128)S(1)}, f32[4,128]{1,0:T(4,128)}, u32[]{:S(2)}) copy-start(f32[4,128]{1,0:T(4,128)} %copy-done.27) | copy-start | bytes 6148
  230.9 78.9 %copy-start.35 = (f32[256]{0:T(256)S(1)}, f32[256]{0:T(256)}, u32[]{:S(2)}) copy-start(f32[256]{0:T(256)} %copy-done.34) | copy-start | bytes 3076
  258.5 51.5 %copy-start.33 = (f32[4,128]{1,0:T(4,128)S(1)}, f32[4,128]{1,0:T(4,128)}, u32[]{:S(2)}) copy-start(f32[4,128]{1,0:T(4,128)} %copy-done.32) | copy-start | bytes 6148
  258.5 213.1 %reduce-scatter.28.cloned.1.call-start = ((), (), s32[]{:S(2)}) async-start(), calls=%async_computation.16 | async-start | bytes 2457600
  309.7 1.6 copy-start.9
  311.5 2.5 copy-start.25
  319.0 52.1 %copy-start.41 = (u32[32]{0:T(128)S(1)}, u32[32]{0:T(128)}, u32[]{:S(2)}) copy-start(u32[32]{0:T(128)} %constant.85) | copy-start | bytes 388
  319.0 52.7 %copy-start.40 = (u32[32]{0:T(128)S(1)}, u32[32]{0:T(128)}, u32[]{:S(2)}) copy-start(u32[32]{0:T(128)} %constant.89) | copy-start | bytes 388
  319.0 54.5 %copy-start.30 = (f32[4,128]{1,0:T(4,128)S(1)}, f32[4,128]{1,0:T(4,128)}, u32[]{:S(2)}) copy-start(f32[4,128]{1,0:T(4,128)} %copy-done.29) | copy-start | bytes 6148
  319.0 154.7 %copy-start.5 = (bf16[4,128,640]{2,1,0:T(8,128)(2,1)S(1)}, bf16[4,128,640]{2,1,0:T(8,128)(2,1)}, u32[]{:S(2)}) copy-start(bf16[4,128,640]{2,1,0:T(8,128)(2,1)} %param.8) | copy-start | bytes 1966084
  319.0 188.4 %reduce-scatter.24.cloned.1.call-start = ((), (), s32[]{:S(2)}) async-start(), calls=%async_computation.14 | async-start | bytes 1474560 | tf_op jit(solution)/shard_map/reduce_scatter | solution.py:347
  371.0 167.7 %reduce-scatter.18.cloned.1.call-start = ((), (), s32[]{:S(2)}) async-start(), calls=%async_computation.11 | async-start | bytes 552960 | tf_op jit(solution)/shard_map/reduce_scatter | solution.py:341
  473.7 30.1 %copy-start.2 = (f32[512,640]{1,0:T(8,128)S(1)}, f32[512,640]{1,0:T(8,128)}, u32[]{:S(2)}) copy-start(f32[512,640]{1,0:T(8,128)} %copy-done.1) | copy-start | bytes 3932164
Sparse Core Ops, SparseCore 0:
  87.3 56.4 all-gather.1
  185.6 28.0 reduce-scatter.19
  216.7 39.5 reduce-scatter.25
  258.4 50.0 reduce-scatter.15
  311.3 59.5 reduce-scatter.21
  373.6 30.4 reduce-scatter.29
  406.5 29.3 reduce-scatter.31
  439.4 32.2 reduce-scatter.27
  474.0 33.3 reduce-scatter.23
  509.6 29.0 reduce-scatter.17
